TPU v7x, 256 devices: a whole 4x4x8 slice. The times are simulated.
256 devices in a mesh: section: 8 (over z_lo, y), seq: 32 (over x, z_hi, core).
Axes of the slice: x: 4, y: 4, z: 8 (z_hi: 4, z_lo: 2; z = z_hi * 2 + z_lo), core: 2. Of those that a mesh axis runs over, the one named last changes fastest.
Arguments:
- qkv: bfloat16 [8, 4096, 3, 4096], P('section', 'seq'), may hold values from -20 to 20
- scale_exp: int32 [8, 32, 3, 32], P('section', 'seq'), may hold values from -1 to 2
- residual_in: bfloat16 [8, 4096, 4096], P('section', 'seq'), may hold values from -6 to 6
- skip_in: bfloat16 [8, 4096, 4096], P('section', 'seq'), may hold values from -6 to 6
- skip_gain: float32 [4096], replicated, may hold values from 0.1 to 1.9
Outputs:
- combined: bfloat16 [8, 4096, 4096], P('section', 'seq')
All inputs are finite; a program needn't handle non-finite values.
Results may differ from a plain program's by a relative error of at most 0.0045.
Values may be sent and summed in bfloat16 or wider, within the bound.
A program may use at most 64 MiB of HBM per device.

v0:
```python
import math

import jax
import jax.numpy as jnp
from jax import lax
from jax.sharding import PartitionSpec as P


def shifted(value, axis, steps):
    count = lax.axis_size(axis)
    pairs = [(source, (source + steps) % count) for source in range(count)]
    return lax.ppermute(value, axis, pairs)


def from_partner(block, axis, stride):
    count = lax.axis_size(axis)
    route = []
    for low in range(count):
        high = low | 1 << stride
        if high != low and high < count:
            route += [(low, high), (high, low)]
    return lax.ppermute(block, axis, route)


def body(qkv, scale_exp, residual_in, skip_in, skip_gain):
    tok_rows = qkv.shape[1]
    feature_count = qkv.shape[3]
    heads_all = scale_exp.shape[3]
    blocks = scale_exp.shape[1]
    head_size = feature_count // heads_all
    factor = jnp.exp2(scale_exp[0].astype(jnp.float32))
    shaped = qkv[0].reshape(blocks, tok_rows // blocks, 3, heads_all, head_size)
    scaled = (shaped.astype(jnp.float32) * factor[:, None, :, :, None]).astype(jnp.bfloat16)
    scaled = scaled.reshape(tok_rows, 3, heads_all, head_size)
    spread = lax.all_to_all(scaled, "seq", split_axis=2, concat_axis=0, tiled=True)
    all_rows = spread.shape[0]
    heads_here = spread.shape[2]
    block_rows = min(512, all_rows)
    queries = spread[:, 0].reshape(all_rows // block_rows, block_rows, heads_here, head_size)
    key_rows = spread[:, 1]
    value_rows = spread[:, 2]
    score_scale = 1.0 / math.sqrt(head_size)

    def attend(query_block):
        scores = (
            jnp.einsum("qhd,khd->hqk", query_block, key_rows, preferred_element_type=jnp.float32)
            * score_scale
        )
        weights = jax.nn.softmax(scores, axis=-1).astype(jnp.bfloat16)
        return jnp.einsum(
            "hqk,khd->qhd", weights, value_rows, preferred_element_type=jnp.float32
        ).astype(jnp.bfloat16)

    heads_done = lax.map(attend, queries).reshape(all_rows, heads_here, head_size)
    returned = lax.all_to_all(heads_done, "seq", split_axis=0, concat_axis=1, tiled=True)
    attended = returned.reshape(1, tok_rows, feature_count)
    incoming = shifted(residual_in, "section", 1)
    bit_total = lax.axis_size("section").bit_length() - 1
    mirrored = skip_in
    for bit_number in range(bit_total):
        mirrored = from_partner(mirrored, "section", bit_number)
    combined = (
        incoming.astype(jnp.float32)
        + skip_gain * mirrored.astype(jnp.float32)
        + attended.astype(jnp.float32)
    )
    return combined.astype(jnp.bfloat16)


def solution(mesh):
    return jax.shard_map(
        body,
        mesh=mesh,
        in_specs=(
            P("section", "seq", None, None),
            P("section", "seq", None, None),
            P("section", "seq", None),
            P("section", "seq", None),
            P(),
        ),
        out_specs=P("section", "seq", None),
        check_vma=False,
    )
```

profile of v0, /device:TPU:30, one launch (start us, length us, event | category | flops | bytes accessed | tf_op | source)
XLA Modules:
  0.0 222.6 jit_solution(7878321769053962796)
XLA Ops:
  0.0 3.5 %copy.25 = bf16[1,128,3,4096]{1,3,2,0:T(8,128)(2,1)S(1)} copy(bf16[1,128,3,4096]{3,1,2,0:T(8,128)(2,1)} %param.7) | data formatting | bytes 6291456 | tf_op args[0]
  3.5 2.4 %fusion.12 = bf16[128,3,32,128]{0,3,2,1:T(8,128)(2,1)} fusion(bf16[128,3,32,128]{0,3,2,1:T(8,128)(2,1)S(1)} %bitcast.58, f32[3,32]{1,0:T(4,128)S(1)} %bitcast.62), kind=kLoop, calls=%fused_computation.16 | loop fusion | flops 4718592 | bytes 6291840 | tf_op jit(solution)/shard_map/convert_element_type | solution.py:33
  5.9 4.6 %copy.26 = bf16[128,3,32,128]{3,0,1,2:T(8,128)(2,1)} copy(bf16[128,3,32,128]{0,3,2,1:T(8,128)(2,1)} %fusion.12) | data formatting | bytes 6291456 | tf_op jit(solution)/shard_map/convert_element_type | solution.py:33
  10.5 11.6 %all-to-all-start = ((bf16[128,3,32,128]{3,0,1,2:T(8,128)(2,1)}), bf16[128,3,32,128]{3,0,1,2:T(8,128)(2,1)S(1)}, u32[]{:S(2)}, u32[]{:S(2)}) async-start(bf16[128,3,32,128]{3,0,1,2:T(8,128)(2,1)} %copy.26), calls=%async_computation | async-start | bytes 6291456 | tf_op jit(solution)/shard_map/all_to_all | solution.py:35
  22.1 2.3 %copy.24 = bf16[1,128,4096]{1,2,0:T(8,128)(2,1)} copy(bf16[1,128,4096]{2,1,0:T(8,128)(2,1)} %param.10) | data formatting | bytes 2097152 | tf_op args[3]
  25.2 68.0 %all-to-all-done = bf16[128,3,32,128]{3,0,1,2:T(8,128)(2,1)S(1)} async-done(((bf16[128,3,32,128]{3,0,1,2:T(8,128)(2,1)}), bf16[128,3,32,128]{3,0,1,2:T(8,128)(2,1)S(1)}, u32[]{:S(2)}, u32[]{:S(2)}) %all-to-all-start) | async-done | bytes 3145760 | tf_op jit(solution)/shard_map/all_to_all | solution.py:35
  94.8 43.4 %while.10 = (s32[]{:T(128)}, bf16[8,512,1,128]{3,1,2,0:T(8,128)(2,1)S(1)}, bf16[8,512,1,128]{3,1,2,0:T(8,128)(2,1)S(1)}, bf16[4096,1,128]{2,0,1:T(8,128)(2,1)S(1)}, bf16[4096,1,128]{2,0,1:T(8,128)(2,1)}, /*index=5*/s32[]{:T(128)}) while((s32[]{:T(128)}, bf16[8,512,1,128]{3,1,2,0:T(8,128)(2,1)S(1)}, bf16[8,512,1,128]{3,1,2,0:T(8,128)(2,1)S(1)}, ...), condition=%wide.region_3.4_spmd, body=%wide.region_0.3_spmd.sunk | while | flops 1092680704 | bytes 31729768 | solution.py:54
  97.7 2.6 %fusion.19 = bf16[8,512,1,128]{3,1,2,0:T(8,128)(2,1)S(1)} fusion(bf16[8,512,1,128]{3,1,2,0:T(8,128)(2,1)S(1)} %get-tuple-element.110, s32[]{:T(128)} %get-tuple-element.109, f32[512,4096]{1,0:T(8,128)S(1)} %get-tuple-element.101, f32[512]{0:T(512)S(1)} %fusion.18, f32[512]{0:T(512)S(1)} %get-tuple-element.102, bf16[4096,1,128]{2,0,1:T(8,128)(2,1)S(1)} %copy-done.2), kind=kOutput, calls=%fused_computation.7.clone.1 | convolution fusion | flops 545325056 | bytes 9572356 | tf_op jit(solution)/shard_map/while/body/eval_jaxpr/hqk,khd->qhd/dot_general | solution.py:50
  103.1 2.6 %fusion.19 = bf16[8,512,1,128]{3,1,2,0:T(8,128)(2,1)S(1)} fusion(bf16[8,512,1,128]{3,1,2,0:T(8,128)(2,1)S(1)} %get-tuple-element.110, s32[]{:T(128)} %get-tuple-element.109, f32[512,4096]{1,0:T(8,128)S(1)} %get-tuple-element.101, f32[512]{0:T(512)S(1)} %fusion.18, f32[512]{0:T(512)S(1)} %get-tuple-element.102, bf16[4096,1,128]{2,0,1:T(8,128)(2,1)S(1)} %copy-done.2), kind=kOutput, calls=%fused_computation.7.clone.1 | convolution fusion | flops 545325056 | bytes 9572356 | tf_op jit(solution)/shard_map/while/body/eval_jaxpr/hqk,khd->qhd/dot_general | solution.py:50
  108.5 2.6 %fusion.19 = bf16[8,512,1,128]{3,1,2,0:T(8,128)(2,1)S(1)} fusion(bf16[8,512,1,128]{3,1,2,0:T(8,128)(2,1)S(1)} %get-tuple-element.110, s32[]{:T(128)} %get-tuple-element.109, f32[512,4096]{1,0:T(8,128)S(1)} %get-tuple-element.101, f32[512]{0:T(512)S(1)} %fusion.18, f32[512]{0:T(512)S(1)} %get-tuple-element.102, bf16[4096,1,128]{2,0,1:T(8,128)(2,1)S(1)} %copy-done.2), kind=kOutput, calls=%fused_computation.7.clone.1 | convolution fusion | flops 545325056 | bytes 9572356 | tf_op jit(solution)/shard_map/while/body/eval_jaxpr/hqk,khd->qhd/dot_general | solution.py:50
  113.9 2.6 %fusion.19 = bf16[8,512,1,128]{3,1,2,0:T(8,128)(2,1)S(1)} fusion(bf16[8,512,1,128]{3,1,2,0:T(8,128)(2,1)S(1)} %get-tuple-element.110, s32[]{:T(128)} %get-tuple-element.109, f32[512,4096]{1,0:T(8,128)S(1)} %get-tuple-element.101, f32[512]{0:T(512)S(1)} %fusion.18, f32[512]{0:T(512)S(1)} %get-tuple-element.102, bf16[4096,1,128]{2,0,1:T(8,128)(2,1)S(1)} %copy-done.2), kind=kOutput, calls=%fused_computation.7.clone.1 | convolution fusion | flops 545325056 | bytes 9572356 | tf_op jit(solution)/shard_map/while/body/eval_jaxpr/hqk,khd->qhd/dot_general | solution.py:50
  119.4 2.6 %fusion.19 = bf16[8,512,1,128]{3,1,2,0:T(8,128)(2,1)S(1)} fusion(bf16[8,512,1,128]{3,1,2,0:T(8,128)(2,1)S(1)} %get-tuple-element.110, s32[]{:T(128)} %get-tuple-element.109, f32[512,4096]{1,0:T(8,128)S(1)} %get-tuple-element.101, f32[512]{0:T(512)S(1)} %fusion.18, f32[512]{0:T(512)S(1)} %get-tuple-element.102, bf16[4096,1,128]{2,0,1:T(8,128)(2,1)S(1)} %copy-done.2), kind=kOutput, calls=%fused_computation.7.clone.1 | convolution fusion | flops 545325056 | bytes 9572356 | tf_op jit(solution)/shard_map/while/body/eval_jaxpr/hqk,khd->qhd/dot_general | solution.py:50
  124.8 2.6 %fusion.19 = bf16[8,512,1,128]{3,1,2,0:T(8,128)(2,1)S(1)} fusion(bf16[8,512,1,128]{3,1,2,0:T(8,128)(2,1)S(1)} %get-tuple-element.110, s32[]{:T(128)} %get-tuple-element.109, f32[512,4096]{1,0:T(8,128)S(1)} %get-tuple-element.101, f32[512]{0:T(512)S(1)} %fusion.18, f32[512]{0:T(512)S(1)} %get-tuple-element.102, bf16[4096,1,128]{2,0,1:T(8,128)(2,1)S(1)} %copy-done.2), kind=kOutput, calls=%fused_computation.7.clone.1 | convolution fusion | flops 545325056 | bytes 9572356 | tf_op jit(solution)/shard_map/while/body/eval_jaxpr/hqk,khd->qhd/dot_general | solution.py:50
  130.2 2.6 %fusion.19 = bf16[8,512,1,128]{3,1,2,0:T(8,128)(2,1)S(1)} fusion(bf16[8,512,1,128]{3,1,2,0:T(8,128)(2,1)S(1)} %get-tuple-element.110, s32[]{:T(128)} %get-tuple-element.109, f32[512,4096]{1,0:T(8,128)S(1)} %get-tuple-element.101, f32[512]{0:T(512)S(1)} %fusion.18, f32[512]{0:T(512)S(1)} %get-tuple-element.102, bf16[4096,1,128]{2,0,1:T(8,128)(2,1)S(1)} %copy-done.2), kind=kOutput, calls=%fused_computation.7.clone.1 | convolution fusion | flops 545325056 | bytes 9572356 | tf_op jit(solution)/shard_map/while/body/eval_jaxpr/hqk,khd->qhd/dot_general | solution.py:50
  135.6 2.6 %fusion.19 = bf16[8,512,1,128]{3,1,2,0:T(8,128)(2,1)S(1)} fusion(bf16[8,512,1,128]{3,1,2,0:T(8,128)(2,1)S(1)} %get-tuple-element.110, s32[]{:T(128)} %get-tuple-element.109, f32[512,4096]{1,0:T(8,128)S(1)} %get-tuple-element.101, f32[512]{0:T(512)S(1)} %fusion.18, f32[512]{0:T(512)S(1)} %get-tuple-element.102, bf16[4096,1,128]{2,0,1:T(8,128)(2,1)S(1)} %copy-done.2), kind=kOutput, calls=%fused_computation.7.clone.1 | convolution fusion | flops 545325056 | bytes 9572356 | tf_op jit(solution)/shard_map/while/body/eval_jaxpr/hqk,khd->qhd/dot_general | solution.py:50
  141.3 7.4 %all-to-all-start.1 = ((bf16[32,2,8192]{2,1,0:T(2,128)(2,1)}), bf16[32,2,8192]{2,1,0:T(2,128)(2,1)S(1)}, u32[]{:S(2)}, u32[]{:S(2)}) async-start(bf16[32,2,8192]{2,1,0:T(2,128)(2,1)} %reshape.85), calls=%async_computation.1 | async-start | bytes 2097152 | tf_op jit(solution)/shard_map/all_to_all | solution.py:55
  151.4 3.5 %collective-permute-start = (bf16[1,128,4096]{1,2,0:T(8,128)(2,1)}, bf16[1,128,4096]{1,2,0:T(8,128)(2,1)}, u32[]{:S(2)}, u32[]{:S(2)}) collective-permute-start(bf16[1,128,4096]{1,2,0:T(8,128)(2,1)} %copy.23), channel_id=1, source_target_pairs={{0,32},{32,64},{64,96},{96,128},{128,160},{160,192},{192,224},{224... | collective-permute-start | bytes 3145736 | tf_op jit(solution)/shard_map/ppermute | solution.py:12
  154.9 21.0 %collective-permute-done.2 = bf16[1,128,4096]{1,2,0:T(8,128)(2,1)} collective-permute-done((bf16[1,128,4096]{1,2,0:T(8,128)(2,1)}, bf16[1,128,4096]{1,2,0:T(8,128)(2,1)}, u32[]{:S(2)}, u32[]{:S(2)}) %collective-permute-start.2) | collective-permute-done | bytes 1048608 | tf_op jit(solution)/shard_map/ppermute | solution.py:22
  175.9 1.9 collective-permute-start.3
  179.0 1.6 convert_bitcast_fusion
  180.5 1.9 copy.31
  182.5 13.4 %collective-permute-done = bf16[1,128,4096]{1,2,0:T(8,128)(2,1)} collective-permute-done((bf16[1,128,4096]{1,2,0:T(8,128)(2,1)}, bf16[1,128,4096]{1,2,0:T(8,128)(2,1)}, u32[]{:S(2)}, u32[]{:S(2)}) %collective-permute-start) | collective-permute-done | bytes 1048608 | tf_op jit(solution)/shard_map/ppermute | solution.py:12
  195.9 23.4 %collective-permute-done.3 = bf16[1,128,4096]{1,2,0:T(8,128)(2,1)} collective-permute-done((bf16[1,128,4096]{1,2,0:T(8,128)(2,1)}, bf16[1,128,4096]{1,2,0:T(8,128)(2,1)}, u32[]{:S(2)}, u32[]{:S(2)}) %collective-permute-start.3) | collective-permute-done | bytes 1048608 | tf_op jit(solution)/shard_map/ppermute | solution.py:22
  219.3 2.0 fusion.13
  (56 shorter events, 33.3 us)
Async XLA Ops:
  0.0 3.5 %copy-start.4 = (s32[1,1,3,32]{3,1,2,0:T(1,128)S(1)}, s32[1,1,3,32]{3,1,2,0:T(1,128)}, u32[]{:S(2)}) copy-start(s32[1,1,3,32]{3,1,2,0:T(1,128)} %param.8) | copy-start | bytes 1156
  10.5 82.6 %all-to-all-start = ((bf16[128,3,32,128]{3,0,1,2:T(8,128)(2,1)}), bf16[128,3,32,128]{3,0,1,2:T(8,128)(2,1)S(1)}, u32[]{:S(2)}, u32[]{:S(2)}) async-start(bf16[128,3,32,128]{3,0,1,2:T(8,128)(2,1)} %copy.26), calls=%async_computation | async-start | bytes 6291456 | tf_op jit(solution)/shard_map/all_to_all | solution.py:35
  24.4 124.3 %collective-permute-start.1 = (bf16[1,128,4096]{1,2,0:T(8,128)(2,1)}, bf16[1,128,4096]{1,2,0:T(8,128)(2,1)}, u32[]{:S(2)}, u32[]{:S(2)}) collective-permute-start(bf16[1,128,4096]{1,2,0:T(8,128)(2,1)} %copy.24), channel_id=1, source_target_pairs={{0,32},{32,0},{64,96},{96,64},{128,160},{160,128},{192,224},{224,1... | collective-permute-start | bytes 3145736 | tf_op jit(solution)/shard_map/ppermute | solution.py:22
  93.4 1.4 copy-start
  96.2 1.5 copy-start.2
  101.6 1.5 copy-start.2
  107.0 1.5 copy-start.2
  112.4 1.5 copy-start.2
  117.8 1.5 copy-start.2
  123.3 1.5 copy-start.2
  128.7 1.5 copy-start.2
  134.1 1.5 copy-start.2
  138.2 11.9 %copy-start.1 = (bf16[1,128,4096]{2,1,0:T(8,128)(2,1)S(1)}, bf16[1,128,4096]{2,1,0:T(8,128)(2,1)}, u32[]{:S(2)}) copy-start(bf16[1,128,4096]{2,1,0:T(8,128)(2,1)} %param.9) | copy-start | bytes 3145732
  141.3 36.5 %all-to-all-start.1 = ((bf16[32,2,8192]{2,1,0:T(2,128)(2,1)}), bf16[32,2,8192]{2,1,0:T(2,128)(2,1)S(1)}, u32[]{:S(2)}, u32[]{:S(2)}) async-start(bf16[32,2,8192]{2,1,0:T(2,128)(2,1)} %reshape.85), calls=%async_computation.1 | async-start | bytes 2097152 | tf_op jit(solution)/shard_map/all_to_all | solution.py:55
  148.7 27.1 %collective-permute-start.2 = (bf16[1,128,4096]{1,2,0:T(8,128)(2,1)}, bf16[1,128,4096]{1,2,0:T(8,128)(2,1)}, u32[]{:S(2)}, u32[]{:S(2)}) collective-permute-start(bf16[1,128,4096]{1,2,0:T(8,128)(2,1)} %collective-permute-done.1), channel_id=1, source_target_pairs={{0,64},{64,0},{32,96},{96,32},{128,192},{192,128},{160,224},{224,1... | collective-permute-start | bytes 3145736 | tf_op jit(solution)/shard_map/ppermute | solution.py:22
  151.4 67.9 %copy-start.3 = (f32[4096]{0:T(1024)S(1)}, f32[4096]{0:T(1024)}, u32[]{:S(2)}) copy-start(f32[4096]{0:T(1024)} %param.11) | copy-start | bytes 49156
  151.4 44.5 %collective-permute-start = (bf16[1,128,4096]{1,2,0:T(8,128)(2,1)}, bf16[1,128,4096]{1,2,0:T(8,128)(2,1)}, u32[]{:S(2)}, u32[]{:S(2)}) collective-permute-start(bf16[1,128,4096]{1,2,0:T(8,128)(2,1)} %copy.23), channel_id=1, source_target_pairs={{0,32},{32,64},{64,96},{96,128},{128,160},{160,192},{192,224},{224... | collective-permute-start | bytes 3145736 | tf_op jit(solution)/shard_map/ppermute | solution.py:12
  175.9 43.4 %collective-permute-start.3 = (bf16[1,128,4096]{1,2,0:T(8,128)(2,1)}, bf16[1,128,4096]{1,2,0:T(8,128)(2,1)}, u32[]{:S(2)}, u32[]{:S(2)}) collective-permute-start(bf16[1,128,4096]{1,2,0:T(8,128)(2,1)} %collective-permute-done.2), channel_id=1, source_target_pairs={{0,128},{128,0},{32,160},{160,32},{64,192},{192,64},{96,224},{224,... | collective-permute-start | bytes 3145736 | tf_op jit(solution)/shard_map/ppermute | solution.py:22
where the time goes:
time: 223 us
  waiting for transfers between devices  126 us (57%)
  matrix products  31.1 us (14%)
  starting transfers between devices  26.5 us (12%)
  local copies, waits for them, and re-layouts  19.4 us (9%)
  other arithmetic  19.4 us (9%)
    all_to_all x1, waiting for transfers between devices, body(): lax.all_to_all(scaled, 'seq', split_axis=2, concat_axis=0, tiled=True)  68 us
    ppermute x3, waiting for transfers between devices, from_partner(): return lax.ppermute(block, axis, route)  44.4 us
    dot_general x8, matrix products, attend(): jnp.einsum('hqk,khd->qhd', weights, value_rows, preferred_element_type=jn...  20.4 us
    ppermute x1, waiting for transfers between devices, shifted(): return lax.ppermute(value, axis, pairs)  13.4 us
    reduce_sum x8, other arithmetic, attend(): weights = jax.nn.softmax(scores, axis=-1).astype(jnp.bfloat16)  12 us
    all_to_all x1, starting transfers between devices, body(): lax.all_to_all(scaled, 'seq', split_axis=2, concat_axis=0, tiled=True)  11.6 us
    dot_general x8, matrix products, attend(): jnp.einsum('qhd,khd->hqk', query_block, key_rows, preferred_element_type=...  10.7 us
    unnamed x14, local copies, waits for them, and re-layouts  9.48 us
  transfers between devices with their start and end apart: 6, of which 4 were waited for; matrix products, arithmetic and copies ran while one was open for 25% of the time, Pallas kernels for 0%

commit v1 on v0

v1 whole, which is shorter than its diff:
```python
import math

import jax
import jax.numpy as jnp
from jax import lax
from jax.experimental import pallas as pl
from jax.experimental.pallas import tpu as pltpu
from jax.sharding import PartitionSpec as P

MESH = pl.DeviceIdType.MESH
PEERS = 32
HS = 128
ROWS = 128
TOKENS = PEERS * ROWS
HD = PEERS * HS
SECTIONS = 8
GROUP = 2
QB = GROUP * ROWS
KB = 512
LOG2E = math.log2(math.e)
SCORE = LOG2E / math.sqrt(HS)


def pick(i, values):
    out = values[-1]
    for n in range(len(values) - 2, -1, -1):
        out = jnp.where(i == n, values[n], out)
    return out


def offsets(slot):
    return pick((slot // 4) % 4, (2, 1, 3, 0)), pick(slot % 4, (1, 3, 2, 0)), 1 - slot // 16


def target(seq, slot):
    dx, dz, dc = offsets(slot)
    return ((seq // 8 + dx) % 4) * 8 + ((seq // 2 + dz) % 4) * 2 + (seq + dc) % 2


def origin(seq, slot):
    dx, dz, dc = offsets(slot)
    return ((seq // 8 + 4 - dx) % 4) * 8 + ((seq // 2 + 4 - dz) % 4) * 2 + (seq + dc) % 2


def kernel(
    exps, qkv_hbm, res_hbm, skip_hbm, gain, out,
    qkv, kv_out, q_out, kv_in, q_in, o_out, o_in, res_in, skip_in, own_a, own_b, scores,
    load_sem, own_sem, kv_send, kv_recv, q_send, q_recv, o_send, o_recv, res_sem, skip_sem,
):
    sec = lax.axis_index("section")
    seq = lax.axis_index("seq")
    nxt = (sec + 1) % SECTIONS
    prv = (sec + SECTIONS - 1) % SECTIONS
    mir = SECTIONS - 1 - sec
    sums = nxt == mir
    summed = prv == mir

    load = pltpu.make_async_copy(qkv_hbm, qkv, load_sem)
    load.start()
    barrier = pltpu.get_barrier_semaphore()

    def greet(k, _):
        pl.semaphore_signal(barrier, inc=1, device_id=(sec, target(seq, k)), device_id_type=MESH)
        return 0

    lax.fori_loop(0, PEERS - 1, greet, 0)
    for s in (nxt, prv, mir):
        pl.semaphore_signal(barrier, inc=1, device_id=(s, seq), device_id_type=MESH)

    own_res = pltpu.make_async_copy(res_hbm, own_a, own_sem.at[0])
    own_skip = pltpu.make_async_copy(skip_hbm, own_b, own_sem.at[1])
    own_res.start()
    own_skip.start()
    load.wait()

    def scale(k, _):
        head = target(seq, k)
        cols = pl.ds(pl.multiple_of(head * HS, HS), HS)
        for c in range(3):
            power = jnp.left_shift(jnp.int32(1), exps[c, head] + 8).astype(jnp.float32) * (2.0**-8)
            part = (qkv[c, :, cols].astype(jnp.float32) * power).astype(jnp.bfloat16)
            if c == 0:
                q_out[k] = part
            else:
                kv_out[k, c - 1] = part
        return 0

    lax.fori_loop(0, PEERS, scale, 0)
    kv_in[PEERS - 1] = kv_out[PEERS - 1]
    q_in[PEERS - 1] = q_out[PEERS - 1]
    own_res.wait()
    own_skip.wait()

    @pl.when(sums)
    def _():
        def add(i, _):
            rows = pl.ds(pl.multiple_of(i * 16, 16), 16)
            both = own_a[rows, :].astype(jnp.float32) + gain[...] * own_b[rows, :].astype(jnp.float32)
            own_a[rows, :] = both.astype(jnp.bfloat16)
            return 0

        lax.fori_loop(0, ROWS // 16, add, 0)

    pl.semaphore_wait(barrier, PEERS - 1 + 3)

    def kv_copy(k):
        return pltpu.make_async_remote_copy(
            src_ref=kv_out.at[k], dst_ref=kv_in.at[k], send_sem=kv_send.at[k], recv_sem=kv_recv.at[k],
            device_id=(sec, target(seq, k)), device_id_type=MESH,
        )

    def q_copy(k):
        return pltpu.make_async_remote_copy(
            src_ref=q_out.at[k], dst_ref=q_in.at[k], send_sem=q_send.at[k], recv_sem=q_recv.at[k],
            device_id=(sec, target(seq, k)), device_id_type=MESH,
        )

    def o_copy(k):
        return pltpu.make_async_remote_copy(
            src_ref=o_out.at[k], dst_ref=o_in.at[k], send_sem=o_send.at[k], recv_sem=o_recv.at[k],
            device_id=(sec, origin(seq, k)), device_id_type=MESH,
        )

    res_copy = pltpu.make_async_remote_copy(
        src_ref=own_a, dst_ref=res_in, send_sem=res_sem.at[0], recv_sem=res_sem.at[1],
        device_id=(nxt, seq), device_id_type=MESH,
    )

    def skip_copy(i):
        rows = pl.ds(pl.multiple_of(i * 16, 16), 16)
        return pltpu.make_async_remote_copy(
            src_ref=own_b.at[rows], dst_ref=skip_in.at[rows], send_sem=skip_sem.at[0, i], recv_sem=skip_sem.at[1, i],
            device_id=(mir, seq), device_id_type=MESH,
        )

    def start_kv(k, _):
        kv_copy(k).start()
        return 0

    def start_q(k, _):
        q_copy(k).start()
        return 0

    lax.fori_loop(0, PEERS - 1, start_kv, 0)
    res_copy.start()
    lax.fori_loop(0, PEERS - 1, start_q, 0)

    def take_kv(k, _):
        kv_copy(k).wait_recv()
        return 0

    lax.fori_loop(0, PEERS - 1, take_kv, 0)

    def attend(g, _):
        first = g * GROUP
        for n in range(GROUP):

            @pl.when(first + n < PEERS - 1)
            def _():
                q_copy(first + n).wait_recv()

        q = q_in[pl.ds(first, GROUP)].reshape(QB, HS)
        most = None
        for j in range(TOKENS // KB):
            keys = kv_in[j * KB // ROWS : (j + 1) * KB // ROWS, 0].reshape(KB, HS)
            s = lax.dot_general(q, keys, (((1,), (1,)), ((), ())), preferred_element_type=jnp.float32)
            scores[:, j * KB : (j + 1) * KB] = s
            for u in range(KB // 128):
                t = s[:, u * 128 : (u + 1) * 128]
                most = t if most is None else jnp.maximum(most, t)
        top = jnp.max(most, axis=1, keepdims=True) * SCORE
        acc = jnp.zeros((QB, HS), jnp.float32)
        total = jnp.zeros((QB, 128), jnp.float32)
        for j in range(TOKENS // KB):
            values = kv_in[j * KB // ROWS : (j + 1) * KB // ROWS, 1].reshape(KB, HS)
            p = jnp.exp2(scores[:, j * KB : (j + 1) * KB] * SCORE - top)
            for u in range(KB // 128):
                total = total + p[:, u * 128 : (u + 1) * 128]
            acc = acc + jnp.dot(p.astype(jnp.bfloat16), values, preferred_element_type=jnp.float32)
        done = (acc / jnp.sum(total, axis=1, keepdims=True)).astype(jnp.bfloat16)
        o_out[pl.ds(first, GROUP)] = done.reshape(GROUP, ROWS, HS)
        for n in range(GROUP):

            @pl.when(first + n < PEERS - 1)
            def _():
                o_copy(first + n).start()

        @pl.when(jnp.logical_and(g < 8, jnp.logical_not(sums)))
        def _():
            skip_copy(g).start()

        return 0

    lax.fori_loop(0, PEERS // GROUP, attend, 0)
    o_in[PEERS - 1] = o_out[PEERS - 1]

    res_copy.wait_recv()

    @pl.when(jnp.logical_not(summed))
    def _():
        def take_skip(i, _):
            skip_copy(i).wait_recv()
            return 0

        lax.fori_loop(0, 8, take_skip, 0)

    def finish(k, _):
        @pl.when(k < PEERS - 1)
        def _():
            o_copy(k).wait_recv()

        cols = pl.ds(pl.multiple_of(target(seq, k) * HS, HS), HS)
        base = res_in[:, cols].astype(jnp.float32)

        @pl.when(summed)
        def _():
            out[:, cols] = (base + o_in[k].astype(jnp.float32)).astype(jnp.bfloat16)

        @pl.when(jnp.logical_not(summed))
        def _():
            both = base + gain[:, cols] * skip_in[:, cols].astype(jnp.float32)
            out[:, cols] = (both + o_in[k].astype(jnp.float32)).astype(jnp.bfloat16)

        return 0

    lax.fori_loop(0, PEERS, finish, 0)

    def sent(k, _):
        kv_copy(k).wait_send()
        q_copy(k).wait_send()
        o_copy(k).wait_send()
        return 0

    lax.fori_loop(0, PEERS - 1, sent, 0)
    res_copy.wait_send()

    @pl.when(jnp.logical_not(sums))
    def _():
        def sent_skip(i, _):
            skip_copy(i).wait_send()
            return 0

        lax.fori_loop(0, 8, sent_skip, 0)


def body(qkv, scale_exp, residual_in, skip_in, skip_gain):
    bf16 = jnp.bfloat16
    block = pltpu.VMEM((PEERS, ROWS, HS), bf16)
    pair = pltpu.VMEM((PEERS, 2, ROWS, HS), bf16)
    rows = pltpu.VMEM((ROWS, HD), bf16)
    sems = pltpu.SemaphoreType.DMA((PEERS,))
    anywhere = pl.BlockSpec(memory_space=pl.ANY)
    vmem = pl.BlockSpec(memory_space=pltpu.VMEM)
    combined = pl.pallas_call(
        kernel,
        out_shape=jax.ShapeDtypeStruct((ROWS, HD), bf16),
        in_specs=[pl.BlockSpec(memory_space=pltpu.SMEM), anywhere, anywhere, anywhere, vmem],
        out_specs=vmem,
        scratch_shapes=[
            pltpu.VMEM((3, ROWS, HD), bf16), pair, block, pair, block, block, block, rows, rows, rows, rows,
            pltpu.VMEM((QB, TOKENS), jnp.float32),
            pltpu.SemaphoreType.DMA, pltpu.SemaphoreType.DMA((2,)), sems, sems, sems, sems, sems, sems,
            pltpu.SemaphoreType.DMA((2,)), pltpu.SemaphoreType.DMA((2, 8)),
        ],
        compiler_params=pltpu.CompilerParams(
            collective_id=0, has_side_effects=True, vmem_limit_bytes=56 * 2**20
        ),
    )(
        scale_exp.reshape(3, PEERS),
        qkv[0].transpose(1, 0, 2),
        residual_in[0],
        skip_in[0],
        skip_gain.reshape(1, HD),
    )
    return combined[None]


def solution(mesh):
    return jax.shard_map(
        body,
        mesh=mesh,
        in_specs=(
            P("section", "seq", None, None),
            P("section", "seq", None, None),
            P("section", "seq", None),
            P("section", "seq", None),
            P(),
        ),
        out_specs=P("section", "seq", None),
        check_vma=False,
    )
```

time: 223 us -> 135 us (0.61)
  the two profiles are of different devices: /device:TPU:30 before, /device:TPU:25 now
where the time goes in v1:
time: 135 us
  Pallas kernels  131 us (97%)
  local copies, waits for them, and re-layouts  3.55 us (3%)
    pallas_call x1, Pallas kernels, body(): pl.pallas_call(kernel, out_shape=jax.ShapeDtypeStruct((ROWS, HD), bf16),...  131 us
    unnamed x2, local copies, waits for them, and re-layouts  3.55 us

profile of v1, /device:TPU:25, one launch (start us, length us, event | category | flops | bytes accessed | tf_op | source)
XLA Modules:
  0.0 134.7 jit_solution(13534121140773947189)
XLA Ops:
  0.0 1.3 copy.8
  1.3 131.1 %shard_map.55 = bf16[128,4096]{1,0:T(8,128)(2,1)} custom-call(s32[3,32]{1,0:T(4,128)} %bitcast.15, bf16[3,128,4096]{2,1,0:T(8,128)(2,1)} %bitcast.11, bf16[128,4096]{1,0:T(8,128)(2,1)} %bitcast.12, bf16[128,4096]{1,0:T(8,128)(2,1)} %bitcast.13, f32[1,4096]{1,0:T(1,128)} %bitcast.14), custom_call_target="tpu_custom_call" | custom-call | tf_op jit(solution)/shard_map/pallas_call | solution.py:254
  132.4 2.3 %copy.10 = bf16[1,128,4096]{2,1,0:T(8,128)(2,1)} copy(bf16[1,128,4096]{2,1,0:T(8,128)(2,1)} %bitcast.10) | data formatting | bytes 2097152

commit v2 on v1

--- a/solution.py
+++ b/solution.py
@@ -14,6 +14,10 @@
 TOKENS = PEERS * ROWS
 HD = PEERS * HS
 SECTIONS = 8
+RELAYED = 16
+LAG = 10
+CHUNK_GROUP = 4
+CHUNKS = 8
 GROUP = 2
 QB = GROUP * ROWS
 KB = 512
@@ -29,29 +33,35 @@
 
 
 def offsets(slot):
-    return pick((slot // 4) % 4, (2, 1, 3, 0)), pick(slot % 4, (1, 3, 2, 0)), 1 - slot // 16
-
-
-def target(seq, slot):
+    dz = jnp.where(slot < RELAYED, 2 - slot % 2, 3 - 3 * (slot % 2))
+    return pick((slot // 2) % 4, (2, 1, 3, 0)), dz, 1 - (slot // 8) % 2
+
+
+def shifted(seq, slot, sign, way):
     dx, dz, dc = offsets(slot)
-    return ((seq // 8 + dx) % 4) * 8 + ((seq // 2 + dz) % 4) * 2 + (seq + dc) % 2
-
-
-def origin(seq, slot):
-    dx, dz, dc = offsets(slot)
-    return ((seq // 8 + 4 - dx) % 4) * 8 + ((seq // 2 + 4 - dz) % 4) * 2 + (seq + dc) % 2
+    x, z, core = seq // 8, (seq // 2) % 4, seq % 2
+    return ((x + 4 + way * dx) % 4) * 8 + ((z + 4 + way * sign * dz) % 4) * 2 + (core + dc) % 2
+
+
+def target(seq, slot, sign):
+    return shifted(seq, slot, sign, 1)
+
+
+def origin(seq, slot, sign):
+    return shifted(seq, slot, sign, -1)
 
 
 def kernel(
     exps, qkv_hbm, res_hbm, skip_hbm, gain, out,
-    qkv, kv_out, q_out, kv_in, q_in, o_out, o_in, res_in, skip_in, own_a, own_b, scores,
-    load_sem, own_sem, kv_send, kv_recv, q_send, q_recv, o_send, o_recv, res_sem, skip_sem,
+    qkv, kv_out, q_out, kv_in, q_in, o_out, o_in, passed, res_in, skip_in, own_a, own_b, both, scores,
+    load_sem, own_sem, kv_send, kv_recv, q_send, q_recv, o_send, o_recv, pass_send, res_sem, skip_sem,
 ):
     sec = lax.axis_index("section")
     seq = lax.axis_index("seq")
     nxt = (sec + 1) % SECTIONS
     prv = (sec + SECTIONS - 1) % SECTIONS
     mir = SECTIONS - 1 - sec
+    sign = 1 - 2 * (sec // 4)
     sums = nxt == mir
     summed = prv == mir
 
@@ -60,10 +70,15 @@
     barrier = pltpu.get_barrier_semaphore()
 
     def greet(k, _):
-        pl.semaphore_signal(barrier, inc=1, device_id=(sec, target(seq, k)), device_id_type=MESH)
+        pl.semaphore_signal(barrier, inc=1, device_id=(sec, target(seq, k, sign)), device_id_type=MESH)
+        return 0
+
+    def greet_relay(k, _):
+        pl.semaphore_signal(barrier, inc=1, device_id=(mir, origin(seq, k, sign)), device_id_type=MESH)
         return 0
 
     lax.fori_loop(0, PEERS - 1, greet, 0)
+    lax.fori_loop(0, RELAYED, greet_relay, 0)
     for s in (nxt, prv, mir):
         pl.semaphore_signal(barrier, inc=1, device_id=(s, seq), device_id_type=MESH)
 
@@ -74,7 +89,7 @@
     load.wait()
 
     def scale(k, _):
-        head = target(seq, k)
+        head = target(seq, k, sign)
         cols = pl.ds(pl.multiple_of(head * HS, HS), HS)
         for c in range(3):
             power = jnp.left_shift(jnp.int32(1), exps[c, head] + 8).astype(jnp.float32) * (2.0**-8)
@@ -95,46 +110,73 @@
     def _():
         def add(i, _):
             rows = pl.ds(pl.multiple_of(i * 16, 16), 16)
-            both = own_a[rows, :].astype(jnp.float32) + gain[...] * own_b[rows, :].astype(jnp.float32)
-            own_a[rows, :] = both.astype(jnp.bfloat16)
+            total = own_a[rows, :].astype(jnp.float32) + gain[...] * own_b[rows, :].astype(jnp.float32)
+            both[rows, :] = total.astype(jnp.bfloat16)
             return 0
 
         lax.fori_loop(0, ROWS // 16, add, 0)
 
-    pl.semaphore_wait(barrier, PEERS - 1 + 3)
+    pl.semaphore_wait(barrier, PEERS - 1 + RELAYED + 3)
 
     def kv_copy(k):
         return pltpu.make_async_remote_copy(
             src_ref=kv_out.at[k], dst_ref=kv_in.at[k], send_sem=kv_send.at[k], recv_sem=kv_recv.at[k],
-            device_id=(sec, target(seq, k)), device_id_type=MESH,
+            device_id=(sec, target(seq, k, sign)), device_id_type=MESH,
         )
 
     def q_copy(k):
         return pltpu.make_async_remote_copy(
             src_ref=q_out.at[k], dst_ref=q_in.at[k], send_sem=q_send.at[k], recv_sem=q_recv.at[k],
-            device_id=(sec, target(seq, k)), device_id_type=MESH,
+            device_id=(sec, target(seq, k, sign)), device_id_type=MESH,
         )
 
     def o_copy(k):
-        return pltpu.make_async_remote_copy(
-            src_ref=o_out.at[k], dst_ref=o_in.at[k], send_sem=o_send.at[k], recv_sem=o_recv.at[k],
-            device_id=(sec, origin(seq, k)), device_id_type=MESH,
-        )
+        relayed = k < RELAYED
+        land = jnp.where(relayed, PEERS + k, k)
+        return pltpu.make_async_remote_copy(
+            src_ref=o_out.at[k], dst_ref=o_in.at[land], send_sem=o_send.at[k], recv_sem=o_recv.at[land],
+            device_id=(jnp.where(relayed, mir, sec), origin(seq, k, sign)), device_id_type=MESH,
+        )
+
+    def pass_copy(k):
+        return pltpu.make_async_remote_copy(
+            src_ref=passed.at[k], dst_ref=o_in.at[k], send_sem=pass_send.at[k], recv_sem=o_recv.at[k],
+            device_id=(mir, seq), device_id_type=MESH,
+        )
+
+    def arrived(slot):
+        pltpu.make_async_copy(o_in.at[slot], o_in.at[slot], o_recv.at[slot]).wait()
 
     res_copy = pltpu.make_async_remote_copy(
         src_ref=own_a, dst_ref=res_in, send_sem=res_sem.at[0], recv_sem=res_sem.at[1],
         device_id=(nxt, seq), device_id_type=MESH,
     )
 
-    def skip_copy(i):
-        rows = pl.ds(pl.multiple_of(i * 16, 16), 16)
-        return pltpu.make_async_remote_copy(
-            src_ref=own_b.at[rows], dst_ref=skip_in.at[rows], send_sem=skip_sem.at[0, i], recv_sem=skip_sem.at[1, i],
+    def chunk_copy(i, src, dst):
+        z = (seq // 2 + 4 - 3 * sign * (i % 2)) % 4
+        cols = pl.ds(pl.multiple_of(((i // 2) * 8 + z * 2) * HS, 2 * HS), 2 * HS)
+        return pltpu.make_async_remote_copy(
+            src_ref=src.at[:, cols], dst_ref=dst.at[:, cols], send_sem=skip_sem.at[0, i], recv_sem=skip_sem.at[1, i],
             device_id=(mir, seq), device_id_type=MESH,
         )
 
+    def relay(k):
+        arrived(PEERS + k)
+        cols = pl.ds(pl.multiple_of(target(seq, k, -sign) * HS, HS), HS)
+        part = o_in[PEERS + k].astype(jnp.float32) + gain[:, cols] * own_b[:, cols].astype(jnp.float32)
+
+        @pl.when(sums)
+        def _():
+            passed[k] = (part + own_a[:, cols].astype(jnp.float32)).astype(jnp.bfloat16)
+
+        @pl.when(jnp.logical_not(sums))
+        def _():
+            passed[k] = part.astype(jnp.bfloat16)
+
+        pass_copy(k).start()
+
     def start_kv(k, _):
-        kv_copy(k).start()
+        kv_copy((k % 2) * RELAYED + k // 2).start()
         return 0
 
     def start_q(k, _):
@@ -142,7 +184,11 @@
         return 0
 
     lax.fori_loop(0, PEERS - 1, start_kv, 0)
-    res_copy.start()
+
+    @pl.when(jnp.logical_not(sums))
+    def _():
+        res_copy.start()
+
     lax.fori_loop(0, PEERS - 1, start_q, 0)
 
     def take_kv(k, _):
@@ -185,45 +231,65 @@
             def _():
                 o_copy(first + n).start()
 
-        @pl.when(jnp.logical_and(g < 8, jnp.logical_not(sums)))
-        def _():
-            skip_copy(g).start()
+        @pl.when(jnp.logical_and(jnp.logical_and(g >= CHUNK_GROUP, g < CHUNK_GROUP + CHUNKS), sums))
+        def _():
+            chunk_copy(g - CHUNK_GROUP, both, res_in).start()
+
+        @pl.when(jnp.logical_and(jnp.logical_and(g >= CHUNK_GROUP, g < CHUNK_GROUP + CHUNKS), jnp.logical_not(sums)))
+        def _():
+            chunk_copy(g - CHUNK_GROUP, own_b, skip_in).start()
+
+        @pl.when(g >= LAG)
+        def _():
+            for n in range(GROUP):
+                relay((g - LAG) * GROUP + n)
 
         return 0
 
     lax.fori_loop(0, PEERS // GROUP, attend, 0)
+
+    def relay_late(k, _):
+        relay(k)
+        return 0
+
+    lax.fori_loop(PEERS - LAG * GROUP, RELAYED, relay_late, 0)
     o_in[PEERS - 1] = o_out[PEERS - 1]
-
-    res_copy.wait_recv()
 
     @pl.when(jnp.logical_not(summed))
     def _():
-        def take_skip(i, _):
-            skip_copy(i).wait_recv()
-            return 0
-
-        lax.fori_loop(0, 8, take_skip, 0)
+        res_copy.wait_recv()
+
+    def take_chunk(i, _):
+        chunk_copy(i, own_b, skip_in).wait_recv()
+        return 0
+
+    lax.fori_loop(0, CHUNKS, take_chunk, 0)
 
     def finish(k, _):
         @pl.when(k < PEERS - 1)
         def _():
-            o_copy(k).wait_recv()
-
-        cols = pl.ds(pl.multiple_of(target(seq, k) * HS, HS), HS)
-        base = res_in[:, cols].astype(jnp.float32)
-
-        @pl.when(summed)
-        def _():
-            out[:, cols] = (base + o_in[k].astype(jnp.float32)).astype(jnp.bfloat16)
-
-        @pl.when(jnp.logical_not(summed))
-        def _():
-            both = base + gain[:, cols] * skip_in[:, cols].astype(jnp.float32)
-            out[:, cols] = (both + o_in[k].astype(jnp.float32)).astype(jnp.bfloat16)
-
-        return 0
-
-    lax.fori_loop(0, PEERS, finish, 0)
+            arrived(k)
+
+        cols = pl.ds(pl.multiple_of(target(seq, k, sign) * HS, HS), HS)
+        done = o_in[k].astype(jnp.float32)
+
+        @pl.when(jnp.logical_and(summed, k < RELAYED))
+        def _():
+            out[:, cols] = o_in[k]
+
+        @pl.when(jnp.logical_xor(summed, k < RELAYED))
+        def _():
+            out[:, cols] = (res_in[:, cols].astype(jnp.float32) + done).astype(jnp.bfloat16)
+
+        @pl.when(jnp.logical_and(jnp.logical_not(summed), k >= RELAYED))
+        def _():
+            rest = res_in[:, cols].astype(jnp.float32) + gain[:, cols] * skip_in[:, cols].astype(jnp.float32)
+            out[:, cols] = (rest + done).astype(jnp.bfloat16)
+
+        return 0
+
+    lax.fori_loop(RELAYED, PEERS, finish, 0)
+    lax.fori_loop(0, RELAYED, finish, 0)
 
     def sent(k, _):
         kv_copy(k).wait_send()
@@ -231,16 +297,21 @@
         o_copy(k).wait_send()
         return 0
 
+    def sent_more(k, _):
+        pass_copy(k).wait_send()
+        return 0
+
+    def sent_chunk(i, _):
+        chunk_copy(i, own_b, skip_in).wait_send()
+        return 0
+
     lax.fori_loop(0, PEERS - 1, sent, 0)
-    res_copy.wait_send()
+    lax.fori_loop(0, RELAYED, sent_more, 0)
+    lax.fori_loop(0, CHUNKS, sent_chunk, 0)
 
     @pl.when(jnp.logical_not(sums))
     def _():
-        def sent_skip(i, _):
-            skip_copy(i).wait_send()
-            return 0
-
-        lax.fori_loop(0, 8, sent_skip, 0)
+        res_copy.wait_send()
 
 
 def body(qkv, scale_exp, residual_in, skip_in, skip_gain):
@@ -257,10 +328,12 @@
         in_specs=[pl.BlockSpec(memory_space=pltpu.SMEM), anywhere, anywhere, anywhere, vmem],
         out_specs=vmem,
         scratch_shapes=[
-            pltpu.VMEM((3, ROWS, HD), bf16), pair, block, pair, block, block, block, rows, rows, rows, rows,
+            pltpu.VMEM((3, ROWS, HD), bf16), pair, block, pair, block, block,
+            pltpu.VMEM((PEERS + RELAYED, ROWS, HS), bf16), pltpu.VMEM((RELAYED, ROWS, HS), bf16), rows, rows, rows, rows, rows,
             pltpu.VMEM((QB, TOKENS), jnp.float32),
-            pltpu.SemaphoreType.DMA, pltpu.SemaphoreType.DMA((2,)), sems, sems, sems, sems, sems, sems,
-            pltpu.SemaphoreType.DMA((2,)), pltpu.SemaphoreType.DMA((2, 8)),
+            pltpu.SemaphoreType.DMA, pltpu.SemaphoreType.DMA((2,)), sems, sems, sems, sems, sems,
+            pltpu.SemaphoreType.DMA((PEERS + RELAYED,)), pltpu.SemaphoreType.DMA((RELAYED,)),
+            pltpu.SemaphoreType.DMA((2,)), pltpu.SemaphoreType.DMA((2, CHUNKS)),
         ],
         compiler_params=pltpu.CompilerParams(
             collective_id=0, has_side_effects=True, vmem_limit_bytes=56 * 2**20

time: 135 us -> 130 us (0.963)
  the two profiles are of different devices: /device:TPU:25 before, /device:TPU:1 now
where the time goes in v2:
time: 130 us
  Pallas kernels  127 us (98%)
  local copies, waits for them, and re-layouts  3.55 us (3%)
    pallas_call x1, Pallas kernels, body(): pl.pallas_call(kernel, out_shape=jax.ShapeDtypeStruct((ROWS, HD), bf16),...  127 us
    unnamed x2, local copies, waits for them, and re-layouts  3.55 us

profile of v2, /device:TPU:1, one launch (start us, length us, event | category | flops | bytes accessed | tf_op | source)
XLA Modules:
  0.0 130.1 jit_solution(14855185667533498927)
XLA Ops:
  0.0 1.3 copy.8
  1.3 126.5 %shard_map.55 = bf16[128,4096]{1,0:T(8,128)(2,1)} custom-call(s32[3,32]{1,0:T(4,128)} %bitcast.15, bf16[3,128,4096]{2,1,0:T(8,128)(2,1)} %bitcast.11, bf16[128,4096]{1,0:T(8,128)(2,1)} %bitcast.12, bf16[128,4096]{1,0:T(8,128)(2,1)} %bitcast.13, f32[1,4096]{1,0:T(1,128)} %bitcast.14), custom_call_target="tpu_custom_call" | custom-call | tf_op jit(solution)/shard_map/pallas_call | solution.py:325
  127.8 2.3 %copy.10 = bf16[1,128,4096]{2,1,0:T(8,128)(2,1)} copy(bf16[1,128,4096]{2,1,0:T(8,128)(2,1)} %bitcast.10) | data formatting | bytes 2097152

commit v3 on v2

v3 whole, which is shorter than its diff:
```python
import math

import jax
import jax.numpy as jnp
from jax import lax
from jax.experimental import pallas as pl
from jax.experimental.pallas import tpu as pltpu
from jax.sharding import PartitionSpec as P

MESH = pl.DeviceIdType.MESH
PEERS = 32
HS = 128
ROWS = 128
TOKENS = PEERS * ROWS
HD = PEERS * HS
SECTIONS = 8
RELAYED = 16
LAG = 10
CHUNK_GROUP = 4
PARTS = 8
CHUNKS = 8
GROUP = 2
QB = GROUP * ROWS
KB = 512
LOG2E = math.log2(math.e)
SCORE = LOG2E / math.sqrt(HS)


def pick(i, values):
    out = values[-1]
    for n in range(len(values) - 2, -1, -1):
        out = jnp.where(i == n, values[n], out)
    return out


def offsets(slot):
    dz = jnp.where(slot < RELAYED, 2 - slot % 2, 3 - 3 * (slot % 2))
    return pick((slot // 2) % 4, (2, 1, 3, 0)), dz, 1 - (slot // 8) % 2


def shifted(seq, slot, sign, way):
    dx, dz, dc = offsets(slot)
    x, z, core = seq // 8, (seq // 2) % 4, seq % 2
    return ((x + 4 + way * dx) % 4) * 8 + ((z + 4 + way * sign * dz) % 4) * 2 + (core + dc) % 2


def target(seq, slot, sign):
    return shifted(seq, slot, sign, 1)


def origin(seq, slot, sign):
    return shifted(seq, slot, sign, -1)


def pieces(src, dst, sem):
    for i in range(PARTS):
        rows = pl.ds(i * (ROWS // PARTS), ROWS // PARTS)
        pltpu.make_async_copy(src.at[rows], dst.at[rows], sem).start()


def kernel(
    exps, qkv_hbm, res_hbm, skip_hbm, gain, base, o_in,
    qkv, kv_out, q_out, kv_in, q_in, o_out, o_relay, passed, res_in, skip_in, own_a, own_b, both, scores,
    load_sem, own_sem, kv_send, kv_recv, q_send, q_recv, o_send, o_recv, relay_recv, pass_send, res_sem, skip_sem,
):
    sec = lax.axis_index("section")
    seq = lax.axis_index("seq")
    nxt = (sec + 1) % SECTIONS
    prv = (sec + SECTIONS - 1) % SECTIONS
    mir = SECTIONS - 1 - sec
    sign = 1 - 2 * (sec // 4)
    sums = nxt == mir
    summed = prv == mir

    for c in range(3):
        pieces(qkv_hbm.at[c], qkv.at[c], load_sem)
    res_in[...] = jnp.zeros_like(res_in)
    skip_in[...] = jnp.zeros_like(skip_in)
    barrier = pltpu.get_barrier_semaphore()

    def greet(k, _):
        pl.semaphore_signal(barrier, inc=1, device_id=(sec, target(seq, k, sign)), device_id_type=MESH)
        return 0

    def greet_relay(k, _):
        pl.semaphore_signal(barrier, inc=1, device_id=(mir, origin(seq, k, sign)), device_id_type=MESH)
        return 0

    lax.fori_loop(0, PEERS - 1, greet, 0)
    lax.fori_loop(0, RELAYED, greet_relay, 0)
    for s in (nxt, prv, mir):
        pl.semaphore_signal(barrier, inc=1, device_id=(s, seq), device_id_type=MESH)

    pieces(res_hbm, own_a, own_sem.at[0])
    pieces(skip_hbm, own_b, own_sem.at[1])
    pltpu.make_async_copy(qkv_hbm, qkv, load_sem).wait()

    def scale(k, _):
        head = target(seq, k, sign)
        cols = pl.ds(pl.multiple_of(head * HS, HS), HS)
        for c in range(3):
            power = jnp.left_shift(jnp.int32(1), exps[c, 0, head] + 8).astype(jnp.float32) * (2.0**-8)
            part = (qkv[c, :, cols].astype(jnp.float32) * power).astype(jnp.bfloat16)
            if c == 0:
                q_out[k] = part
            else:
                kv_out[k, c - 1] = part
        return 0

    lax.fori_loop(0, PEERS, scale, 0)
    kv_in[PEERS - 1] = kv_out[PEERS - 1]
    q_in[PEERS - 1] = q_out[PEERS - 1]
    pl.semaphore_wait(barrier, PEERS - 1 + RELAYED + 3)

    def kv_copy(k):
        return pltpu.make_async_remote_copy(
            src_ref=kv_out.at[k], dst_ref=kv_in.at[k], send_sem=kv_send.at[k], recv_sem=kv_recv.at[k],
            device_id=(sec, target(seq, k, sign)), device_id_type=MESH,
        )

    def q_copy(k):
        return pltpu.make_async_remote_copy(
            src_ref=q_out.at[k], dst_ref=q_in.at[k], send_sem=q_send.at[k], recv_sem=q_recv.at[k],
            device_id=(sec, target(seq, k, sign)), device_id_type=MESH,
        )

    def columns(k):
        return pl.ds(pl.multiple_of(target(seq, k, sign) * HS, HS), HS)

    def o_copy(k):
        return pltpu.make_async_remote_copy(
            src_ref=o_out.at[k], dst_ref=o_in.at[:, pl.ds(pl.multiple_of(seq * HS, HS), HS)],
            send_sem=o_send.at[k], recv_sem=o_recv.at[k],
            device_id=(sec, origin(seq, k, sign)), device_id_type=MESH,
        )

    def o_copy_relayed(k):
        return pltpu.make_async_remote_copy(
            src_ref=o_out.at[k], dst_ref=o_relay.at[k], send_sem=o_send.at[k], recv_sem=relay_recv.at[k],
            device_id=(mir, origin(seq, k, sign)), device_id_type=MESH,
        )

    def pass_copy(k):
        cols = pl.ds(pl.multiple_of(target(seq, k, -sign) * HS, HS), HS)
        return pltpu.make_async_remote_copy(
            src_ref=passed.at[k], dst_ref=o_in.at[:, cols], send_sem=pass_send.at[k], recv_sem=o_recv.at[k],
            device_id=(mir, seq), device_id_type=MESH,
        )

    res_copy = pltpu.make_async_remote_copy(
        src_ref=own_a, dst_ref=res_in, send_sem=res_sem.at[0], recv_sem=res_sem.at[1],
        device_id=(nxt, seq), device_id_type=MESH,
    )

    def chunk_copy(i, src, dst):
        z = (seq // 2 + 4 - 3 * sign * (i % 2)) % 4
        cols = pl.ds(pl.multiple_of(((i // 2) * 8 + z * 2) * HS, 2 * HS), 2 * HS)
        return pltpu.make_async_remote_copy(
            src_ref=src.at[:, cols], dst_ref=dst.at[:, cols], send_sem=skip_sem.at[0, i], recv_sem=skip_sem.at[1, i],
            device_id=(mir, seq), device_id_type=MESH,
        )

    def relay(k):
        o_copy_relayed(k).wait_recv()
        cols = pl.ds(pl.multiple_of(target(seq, k, -sign) * HS, HS), HS)
        part = o_relay[k].astype(jnp.float32) + gain[:, cols] * own_b[:, cols].astype(jnp.float32)

        @pl.when(sums)
        def _():
            passed[k] = (part + own_a[:, cols].astype(jnp.float32)).astype(jnp.bfloat16)

        @pl.when(jnp.logical_not(sums))
        def _():
            passed[k] = part.astype(jnp.bfloat16)

        pass_copy(k).start()

    def start_kv(k, _):
        kv_copy((k % 2) * RELAYED + k // 2).start()
        return 0

    def start_q(k, _):
        q_copy(k).start()
        return 0

    lax.fori_loop(0, PEERS - 1, start_kv, 0)
    pltpu.make_async_copy(res_hbm, own_a, own_sem.at[0]).wait()
    pltpu.make_async_copy(skip_hbm, own_b, own_sem.at[1]).wait()

    @pl.when(jnp.logical_not(sums))
    def _():
        res_copy.start()

    lax.fori_loop(0, PEERS - 1, start_q, 0)

    @pl.when(sums)
    def _():
        def add(i, _):
            rows = pl.ds(pl.multiple_of(i * 16, 16), 16)
            total = own_a[rows, :].astype(jnp.float32) + gain[...] * own_b[rows, :].astype(jnp.float32)
            both[rows, :] = total.astype(jnp.bfloat16)
            return 0

        lax.fori_loop(0, ROWS // 16, add, 0)

    def take_kv(k, _):
        kv_copy(k).wait_recv()
        return 0

    lax.fori_loop(0, PEERS - 1, take_kv, 0)

    def attend(g, _):
        first = g * GROUP
        for n in range(GROUP):

            @pl.when(first + n < PEERS - 1)
            def _():
                q_copy(first + n).wait_recv()

        q = q_in[pl.ds(first, GROUP)].reshape(QB, HS)
        most = None
        for j in range(TOKENS // KB):
            keys = kv_in[j * KB // ROWS : (j + 1) * KB // ROWS, 0].reshape(KB, HS)
            s = lax.dot_general(q, keys, (((1,), (1,)), ((), ())), preferred_element_type=jnp.float32)
            scores[:, j * KB : (j + 1) * KB] = s
            for u in range(KB // 128):
                t = s[:, u * 128 : (u + 1) * 128]
                most = t if most is None else jnp.maximum(most, t)
        top = jnp.max(most, axis=1, keepdims=True) * SCORE
        acc = jnp.zeros((QB, HS), jnp.float32)
        total = jnp.zeros((QB, 128), jnp.float32)
        for j in range(TOKENS // KB):
            values = kv_in[j * KB // ROWS : (j + 1) * KB // ROWS, 1].reshape(KB, HS)
            p = jnp.exp2(scores[:, j * KB : (j + 1) * KB] * SCORE - top)
            for u in range(KB // 128):
                total = total + p[:, u * 128 : (u + 1) * 128]
            acc = acc + jnp.dot(p.astype(jnp.bfloat16), values, preferred_element_type=jnp.float32)
        done = (acc / jnp.sum(total, axis=1, keepdims=True)).astype(jnp.bfloat16)
        o_out[pl.ds(first, GROUP)] = done.reshape(GROUP, ROWS, HS)
        for n in range(GROUP):

            @pl.when(first + n < RELAYED)
            def _():
                o_copy_relayed(first + n).start()

            @pl.when(jnp.logical_and(first + n >= RELAYED, first + n < PEERS - 1))
            def _():
                o_copy(first + n).start()

        @pl.when(jnp.logical_and(jnp.logical_and(g >= CHUNK_GROUP, g < CHUNK_GROUP + CHUNKS), sums))
        def _():
            chunk_copy(g - CHUNK_GROUP, both, res_in).start()

        @pl.when(jnp.logical_and(jnp.logical_and(g >= CHUNK_GROUP, g < CHUNK_GROUP + CHUNKS), jnp.logical_not(sums)))
        def _():
            chunk_copy(g - CHUNK_GROUP, own_b, skip_in).start()

        @pl.when(g >= LAG)
        def _():
            for n in range(GROUP):
                relay((g - LAG) * GROUP + n)

        return 0

    lax.fori_loop(0, PEERS // GROUP, attend, 0)

    def relay_late(k, _):
        relay(k)
        return 0

    lax.fori_loop(PEERS - LAG * GROUP, RELAYED, relay_late, 0)
    o_in[:, columns(PEERS - 1)] = o_out[PEERS - 1]

    @pl.when(jnp.logical_not(summed))
    def _():
        res_copy.wait_recv()

    def take_chunk(i, _):
        chunk_copy(i, own_b, skip_in).wait_recv()
        return 0

    lax.fori_loop(0, CHUNKS, take_chunk, 0)

    def gather(i, _):
        rows = pl.ds(pl.multiple_of(i * 16, 16), 16)
        base[rows, :] = res_in[rows, :].astype(jnp.float32) + gain[...] * skip_in[rows, :].astype(jnp.float32)
        return 0

    lax.fori_loop(0, ROWS // 16, gather, 0)

    def take_o(k, _):
        o_copy(k).wait_recv()
        return 0

    lax.fori_loop(0, PEERS - 1, take_o, 0)

    def sent(k, _):
        kv_copy(k).wait_send()
        q_copy(k).wait_send()
        o_copy(k).wait_send()
        return 0

    def sent_more(k, _):
        pass_copy(k).wait_send()
        return 0

    def sent_chunk(i, _):
        chunk_copy(i, own_b, skip_in).wait_send()
        return 0

    lax.fori_loop(0, PEERS - 1, sent, 0)
    lax.fori_loop(0, RELAYED, sent_more, 0)
    lax.fori_loop(0, CHUNKS, sent_chunk, 0)

    @pl.when(jnp.logical_not(sums))
    def _():
        res_copy.wait_send()


def body(qkv, scale_exp, residual_in, skip_in, skip_gain):
    bf16 = jnp.bfloat16
    block = pltpu.VMEM((PEERS, ROWS, HS), bf16)
    pair = pltpu.VMEM((PEERS, 2, ROWS, HS), bf16)
    rows = pltpu.VMEM((ROWS, HD), bf16)
    sems = pltpu.SemaphoreType.DMA((PEERS,))
    anywhere = pl.BlockSpec(memory_space=pl.ANY)
    vmem = pl.BlockSpec(memory_space=pltpu.VMEM)
    base, done = pl.pallas_call(
        kernel,
        out_shape=(pltpu.VMEM((ROWS, HD), jnp.float32), rows),
        in_specs=[pl.BlockSpec(memory_space=pltpu.SMEM), anywhere, anywhere, anywhere, vmem],
        out_specs=(vmem, vmem),
        scratch_shapes=[
            pltpu.VMEM((3, ROWS, HD), bf16), pair, block, pair, block, block,
            pltpu.VMEM((RELAYED, ROWS, HS), bf16), pltpu.VMEM((RELAYED, ROWS, HS), bf16), rows, rows, rows, rows, rows,
            pltpu.VMEM((QB, TOKENS), jnp.float32),
            pltpu.SemaphoreType.DMA, pltpu.SemaphoreType.DMA((2,)), sems, sems, sems, sems, sems,
            sems, pltpu.SemaphoreType.DMA((RELAYED,)), pltpu.SemaphoreType.DMA((RELAYED,)),
            pltpu.SemaphoreType.DMA((2,)), pltpu.SemaphoreType.DMA((2, CHUNKS)),
        ],
        compiler_params=pltpu.CompilerParams(
            collective_id=0, has_side_effects=True, vmem_limit_bytes=56 * 2**20
        ),
    )(
        scale_exp[0].transpose(1, 0, 2),
        qkv[0].transpose(1, 0, 2),
        residual_in[0],
        skip_in[0],
        skip_gain.reshape(1, HD),
    )
    return (base + done.astype(jnp.float32)).astype(bf16)[None]


def solution(mesh):
    return jax.shard_map(
        body,
        mesh=mesh,
        in_specs=(
            P("section", "seq", None, None),
            P("section", "seq", None, None),
            P("section", "seq", None),
            P("section", "seq", None),
            P(),
        ),
        out_specs=P("section", "seq", None),
        check_vma=False,
    )
```

time: 130 us -> 127 us (0.977)
  local copies, waits for them, and re-layouts: 3.55 us -> 0 us
  Pallas kernels: 127 us -> 125 us
    unnamed x2 -> x0, local copies, waits for them, and re-layouts: 3.55 us -> none
where the time goes in v3:
time: 127 us
  Pallas kernels  125 us (98%)
    pallas_call x1, Pallas kernels, body(): pl.pallas_call(kernel, out_shape=(pltpu.VMEM((ROWS, HD), jnp.float32), ro...  125 us

profile of v3, /device:TPU:1, one launch (start us, length us, event | category | flops | bytes accessed | tf_op | source)
XLA Modules:
  0.0 126.6 jit_solution(15063166368426396251)
XLA Ops:
  0.0 125.4 %shard_map.55 = (f32[128,4096]{1,0:T(8,128)S(1)}, bf16[128,4096]{1,0:T(8,128)(2,1)S(1)}) custom-call(s32[3,1,32]{2,1,0:T(1,128)} %bitcast.13, bf16[3,128,4096]{2,1,0:T(8,128)(2,1)} %bitcast.9, bf16[128,4096]{1,0:T(8,128)(2,1)} %bitcast.10, bf16[128,4096]{1,0:T(8,128)(2,1)} %bitcast.11, f32[1,4096]{1,0:T(1,128)} %bitcast.12), custom_call_target="tpu_custom_call" | custom-call | tf_op jit(solution)/shard_map/pallas_call | solution.py:328
  125.5 1.2 fusion

commit v4 on v3

--- a/solution.py
+++ b/solution.py
@@ -15,9 +15,9 @@
 HD = PEERS * HS
 SECTIONS = 8
 RELAYED = 16
-LAG = 10
+LAG = 12
 CHUNK_GROUP = 4
-PARTS = 8
+EARLY = 8
 CHUNKS = 8
 GROUP = 2
 QB = GROUP * ROWS
@@ -50,12 +50,6 @@
 
 def origin(seq, slot, sign):
     return shifted(seq, slot, sign, -1)
-
-
-def pieces(src, dst, sem):
-    for i in range(PARTS):
-        rows = pl.ds(i * (ROWS // PARTS), ROWS // PARTS)
-        pltpu.make_async_copy(src.at[rows], dst.at[rows], sem).start()
 
 
 def kernel(
@@ -72,44 +66,43 @@
     sums = nxt == mir
     summed = prv == mir
 
-    for c in range(3):
-        pieces(qkv_hbm.at[c], qkv.at[c], load_sem)
-    res_in[...] = jnp.zeros_like(res_in)
-    skip_in[...] = jnp.zeros_like(skip_in)
+    load = pltpu.make_async_copy(qkv_hbm, qkv, load_sem)
+    own_res = pltpu.make_async_copy(res_hbm, own_a, own_sem.at[0])
+    own_skip = pltpu.make_async_copy(skip_hbm, own_b, own_sem.at[1])
+    load.start()
     barrier = pltpu.get_barrier_semaphore()
 
-    def greet(k, _):
-        pl.semaphore_signal(barrier, inc=1, device_id=(sec, target(seq, k, sign)), device_id_type=MESH)
-        return 0
-
-    def greet_relay(k, _):
-        pl.semaphore_signal(barrier, inc=1, device_id=(mir, origin(seq, k, sign)), device_id_type=MESH)
-        return 0
-
-    lax.fori_loop(0, PEERS - 1, greet, 0)
-    lax.fori_loop(0, RELAYED, greet_relay, 0)
+    for k in range(1, PEERS):
+        pl.semaphore_signal(barrier, inc=1, device_id=(sec, (seq + k) % PEERS), device_id_type=MESH)
+    for a in (1, 2):
+        z = (seq // 2 + 4 - sign * a) % 4
+        for k in range(8):
+            peer = (k // 2) * 8 + z * 2 + k % 2
+            pl.semaphore_signal(barrier, inc=1, device_id=(mir, peer), device_id_type=MESH)
     for s in (nxt, prv, mir):
         pl.semaphore_signal(barrier, inc=1, device_id=(s, seq), device_id_type=MESH)
 
-    pieces(res_hbm, own_a, own_sem.at[0])
-    pieces(skip_hbm, own_b, own_sem.at[1])
-    pltpu.make_async_copy(qkv_hbm, qkv, load_sem).wait()
-
-    def scale(k, _):
+    own_res.start()
+    own_skip.start()
+    load.wait()
+
+    def scaled(k, c):
         head = target(seq, k, sign)
         cols = pl.ds(pl.multiple_of(head * HS, HS), HS)
-        for c in range(3):
-            power = jnp.left_shift(jnp.int32(1), exps[c, 0, head] + 8).astype(jnp.float32) * (2.0**-8)
-            part = (qkv[c, :, cols].astype(jnp.float32) * power).astype(jnp.bfloat16)
-            if c == 0:
-                q_out[k] = part
-            else:
-                kv_out[k, c - 1] = part
-        return 0
-
-    lax.fori_loop(0, PEERS, scale, 0)
-    kv_in[PEERS - 1] = kv_out[PEERS - 1]
-    q_in[PEERS - 1] = q_out[PEERS - 1]
+        power = jnp.left_shift(jnp.int32(1), exps[c, 0, head] + 8).astype(jnp.float32) * (2.0**-8)
+        return (qkv[c, :, cols].astype(jnp.float32) * power).astype(jnp.bfloat16)
+
+    def kv_slot(i):
+        return (i % 2) * RELAYED + i // 2
+
+    def scale_kv(i, _):
+        k = kv_slot(i)
+        kv_out[k, 0] = scaled(k, 1)
+        kv_out[k, 1] = scaled(k, 2)
+        return 0
+
+    lax.fori_loop(0, EARLY, scale_kv, 0)
+
     pl.semaphore_wait(barrier, PEERS - 1 + RELAYED + 3)
 
     def kv_copy(k):
@@ -175,23 +168,32 @@
 
         pass_copy(k).start()
 
-    def start_kv(k, _):
-        kv_copy((k % 2) * RELAYED + k // 2).start()
-        return 0
-
-    def start_q(k, _):
+    def start_kv(i, _):
+        kv_copy(kv_slot(i)).start()
+        return 0
+
+    def scale_start_kv(i, _):
+        scale_kv(i, 0)
+        return start_kv(i, 0)
+
+    def scale_start_q(k, _):
+        q_out[k] = scaled(k, 0)
         q_copy(k).start()
         return 0
 
-    lax.fori_loop(0, PEERS - 1, start_kv, 0)
-    pltpu.make_async_copy(res_hbm, own_a, own_sem.at[0]).wait()
-    pltpu.make_async_copy(skip_hbm, own_b, own_sem.at[1]).wait()
+    lax.fori_loop(0, EARLY, start_kv, 0)
+    lax.fori_loop(EARLY, PEERS - 1, scale_start_kv, 0)
+    own_res.wait()
+    own_skip.wait()
 
     @pl.when(jnp.logical_not(sums))
     def _():
         res_copy.start()
 
-    lax.fori_loop(0, PEERS - 1, start_q, 0)
+    lax.fori_loop(0, PEERS - 1, scale_start_q, 0)
+    kv_in[PEERS - 1, 0] = scaled(PEERS - 1, 1)
+    kv_in[PEERS - 1, 1] = scaled(PEERS - 1, 2)
+    q_in[PEERS - 1] = scaled(PEERS - 1, 0)
 
     @pl.when(sums)
     def _():
@@ -275,46 +277,66 @@
     def _():
         res_copy.wait_recv()
 
-    def take_chunk(i, _):
-        chunk_copy(i, own_b, skip_in).wait_recv()
-        return 0
-
-    lax.fori_loop(0, CHUNKS, take_chunk, 0)
-
-    def gather(i, _):
-        rows = pl.ds(pl.multiple_of(i * 16, 16), 16)
-        base[rows, :] = res_in[rows, :].astype(jnp.float32) + gain[...] * skip_in[rows, :].astype(jnp.float32)
-        return 0
-
-    lax.fori_loop(0, ROWS // 16, gather, 0)
-
-    def take_o(k, _):
-        o_copy(k).wait_recv()
-        return 0
-
-    lax.fori_loop(0, PEERS - 1, take_o, 0)
-
-    def sent(k, _):
+    def sent_early(k, _):
         kv_copy(k).wait_send()
         q_copy(k).wait_send()
-        o_copy(k).wait_send()
-        return 0
-
-    def sent_more(k, _):
-        pass_copy(k).wait_send()
-        return 0
-
-    def sent_chunk(i, _):
-        chunk_copy(i, own_b, skip_in).wait_send()
-        return 0
-
-    lax.fori_loop(0, PEERS - 1, sent, 0)
-    lax.fori_loop(0, RELAYED, sent_more, 0)
-    lax.fori_loop(0, CHUNKS, sent_chunk, 0)
+        return 0
+
+    lax.fori_loop(0, PEERS - 1, sent_early, 0)
 
     @pl.when(jnp.logical_not(sums))
     def _():
         res_copy.wait_send()
+
+    def take_chunk(i, _):
+        chunk_copy(i, own_b, skip_in).wait_recv()
+        return 0
+
+    lax.fori_loop(0, CHUNKS, take_chunk, 0)
+
+    def gather(i, _):
+        step = (sign * (i % 4 - (seq // 2) % 4) + 4) % 4
+        relayed = jnp.logical_or(step == 1, step == 2)
+        cols = pl.ds(pl.multiple_of(i * 2 * HS, 2 * HS), 2 * HS)
+
+        @pl.when(jnp.logical_and(relayed, summed))
+        def _():
+            base[:, cols] = jnp.zeros((ROWS, 2 * HS), jnp.float32)
+
+        @pl.when(jnp.logical_xor(relayed, summed))
+        def _():
+            base[:, cols] = res_in[:, cols].astype(jnp.float32)
+
+        @pl.when(jnp.logical_not(jnp.logical_or(relayed, summed)))
+        def _():
+            base[:, cols] = res_in[:, cols].astype(jnp.float32) + gain[:, cols] * skip_in[:, cols].astype(jnp.float32)
+
+        return 0
+
+    lax.fori_loop(0, PEERS // 2, gather, 0)
+
+    def sent(k, _):
+        o_copy(k).wait_send()
+        return 0
+
+    def sent_more(k, _):
+        pass_copy(k).wait_send()
+        return 0
+
+    def sent_chunk(i, _):
+        chunk_copy(i, own_b, skip_in).wait_send()
+        return 0
+
+    lax.fori_loop(0, CHUNKS, sent_chunk, 0)
+    lax.fori_loop(0, PEERS - 1, sent, 0)
+    lax.fori_loop(0, RELAYED, sent_more, 0)
+
+    def take_o(k, _):
+        o_copy(k).wait_recv()
+        return 0
+
+    lax.fori_loop(RELAYED, PEERS - 1, take_o, 0)
+    lax.fori_loop(0, RELAYED, take_o, 0)
 
 
 def body(qkv, scale_exp, residual_in, skip_in, skip_gain):

time: 127 us -> 124 us (0.976)
  Pallas kernels: 125 us -> 123 us
    pallas_call x1, Pallas kernels: 125 us -> 123 us  [body(): pl.pallas_call(kernel, out_shape=(pltpu.VMEM((ROWS, HD), jnp.float32), ro...]
where the time goes in v4:
time: 124 us
  Pallas kernels  123 us (99%)
    pallas_call x1, Pallas kernels, body(): pl.pallas_call(kernel, out_shape=(pltpu.VMEM((ROWS, HD), jnp.float32), ro...  123 us

profile of v4, /device:TPU:1, one launch (start us, length us, event | category | flops | bytes accessed | tf_op | source)
XLA Modules:
  0.0 123.9 jit_solution(1206117675508836461)
XLA Ops:
  0.0 122.7 %shard_map.55 = (f32[128,4096]{1,0:T(8,128)S(1)}, bf16[128,4096]{1,0:T(8,128)(2,1)S(1)}) custom-call(s32[3,1,32]{2,1,0:T(1,128)} %bitcast.13, bf16[3,128,4096]{2,1,0:T(8,128)(2,1)} %bitcast.9, bf16[128,4096]{1,0:T(8,128)(2,1)} %bitcast.10, bf16[128,4096]{1,0:T(8,128)(2,1)} %bitcast.11, f32[1,4096]{1,0:T(1,128)} %bitcast.12), custom_call_target="tpu_custom_call" | custom-call | tf_op jit(solution)/shard_map/pallas_call | solution.py:350
  122.8 1.2 fusion

commit v5 on v4

--- a/solution.py
+++ b/solution.py
@@ -17,7 +17,7 @@
 RELAYED = 16
 LAG = 12
 CHUNK_GROUP = 4
-EARLY = 8
+EARLY = 3
 CHUNKS = 8
 GROUP = 2
 QB = GROUP * ROWS
@@ -66,10 +66,11 @@
     sums = nxt == mir
     summed = prv == mir
 
-    load = pltpu.make_async_copy(qkv_hbm, qkv, load_sem)
+    load_kv = pltpu.make_async_copy(qkv_hbm.at[pl.ds(1, 2)], qkv.at[pl.ds(1, 2)], load_sem.at[0])
+    load_q = pltpu.make_async_copy(qkv_hbm.at[0], qkv.at[0], load_sem.at[1])
     own_res = pltpu.make_async_copy(res_hbm, own_a, own_sem.at[0])
     own_skip = pltpu.make_async_copy(skip_hbm, own_b, own_sem.at[1])
-    load.start()
+    load_kv.start()
     barrier = pltpu.get_barrier_semaphore()
 
     for k in range(1, PEERS):
@@ -82,9 +83,10 @@
     for s in (nxt, prv, mir):
         pl.semaphore_signal(barrier, inc=1, device_id=(s, seq), device_id_type=MESH)
 
+    load_q.start()
     own_res.start()
     own_skip.start()
-    load.wait()
+    load_kv.wait()
 
     def scaled(k, c):
         head = target(seq, k, sign)
@@ -176,13 +178,19 @@
         scale_kv(i, 0)
         return start_kv(i, 0)
 
-    def scale_start_q(k, _):
+    def q_slot(i):
+        mixed = jnp.where(i % 4 < 3, i - i // 4, RELAYED + i // 4)
+        return jnp.where(i < 20, mixed, jnp.where(i == 20, RELAYED - 1, i))
+
+    def scale_start_q(i, _):
+        k = q_slot(i)
         q_out[k] = scaled(k, 0)
         q_copy(k).start()
         return 0
 
     lax.fori_loop(0, EARLY, start_kv, 0)
     lax.fori_loop(EARLY, PEERS - 1, scale_start_kv, 0)
+    load_q.wait()
     own_res.wait()
     own_skip.wait()
 
@@ -356,7 +364,7 @@
             pltpu.VMEM((3, ROWS, HD), bf16), pair, block, pair, block, block,
             pltpu.VMEM((RELAYED, ROWS, HS), bf16), pltpu.VMEM((RELAYED, ROWS, HS), bf16), rows, rows, rows, rows, rows,
             pltpu.VMEM((QB, TOKENS), jnp.float32),
-            pltpu.SemaphoreType.DMA, pltpu.SemaphoreType.DMA((2,)), sems, sems, sems, sems, sems,
+            pltpu.SemaphoreType.DMA((2,)), pltpu.SemaphoreType.DMA((2,)), sems, sems, sems, sems, sems,
             sems, pltpu.SemaphoreType.DMA((RELAYED,)), pltpu.SemaphoreType.DMA((RELAYED,)),
             pltpu.SemaphoreType.DMA((2,)), pltpu.SemaphoreType.DMA((2, CHUNKS)),
         ],

time: 124 us -> 124 us (level)
  no operation moved by 1% of the time
where the time goes in v5:
time: 124 us
  Pallas kernels  123 us (99%)
    pallas_call x1, Pallas kernels, body(): pl.pallas_call(kernel, out_shape=(pltpu.VMEM((ROWS, HD), jnp.float32), ro...  123 us

profile of v5, /device:TPU:1, one launch (start us, length us, event | category | flops | bytes accessed | tf_op | source)
XLA Modules:
  0.0 123.9 jit_solution(12111584203794640735)
XLA Ops:
  0.0 122.8 %shard_map.55 = (f32[128,4096]{1,0:T(8,128)S(1)}, bf16[128,4096]{1,0:T(8,128)(2,1)S(1)}) custom-call(s32[3,1,32]{2,1,0:T(1,128)} %bitcast.13, bf16[3,128,4096]{2,1,0:T(8,128)(2,1)} %bitcast.9, bf16[128,4096]{1,0:T(8,128)(2,1)} %bitcast.10, bf16[128,4096]{1,0:T(8,128)(2,1)} %bitcast.11, f32[1,4096]{1,0:T(1,128)} %bitcast.12), custom_call_target="tpu_custom_call" | custom-call | tf_op jit(solution)/shard_map/pallas_call | solution.py:358
  122.8 1.2 fusion
